TPU v7x, 32 devices: a whole 2x2x4 slice. The times are simulated.
32 devices in a mesh: groups: 2 (over x), ep: 16 (over z, y, core).
Axes of the slice: x: 2, y: 2, z: 4, core: 2. Of those that a mesh axis runs over, the one named last changes fastest.
Arguments:
- tokens: bfloat16 [256, 3072], P(('groups', 'ep')), parts along dimension 0, may hold values from -6 to 6
- cotangent: bfloat16 [256, 3072], P(('groups', 'ep')), parts along dimension 0, may hold values from -12 to 12
- routes: int32 [256, 4], P(('groups', 'ep')), parts along dimension 0, may hold values from 0 to 15, all different within a row; in each aligned block of 8 rows (0 to 7, 8 to 15, ...) at most 4 rows name the same one
- route_weights: bfloat16 [256, 4], P(('groups', 'ep')), parts along dimension 0, may hold values from 0.049804688 to 0.59765625
- w_gate: bfloat16 [43008, 3072], P('ep'), may hold values from -0.109375 to 0.109375
- w_up: bfloat16 [43008, 3072], P('ep'), may hold values from -0.109375 to 0.109375
- w_down: bfloat16 [43008, 3072], P('ep'), may hold values from -0.078125 to 0.078125
Outputs:
- token_grads: bfloat16 [256, 3072], P(('groups', 'ep')), parts along dimension 0
- grad_gate: bfloat16 [86016, 3072], P(('groups', 'ep')), parts along dimension 0
- grad_up: bfloat16 [86016, 3072], P(('groups', 'ep')), parts along dimension 0
- grad_down: bfloat16 [86016, 3072], P(('groups', 'ep')), parts along dimension 0
There are 2 independent parts, one for each index of `groups`. A program takes and returns all parts, laid end to end along the dimension named above; an argument that names none is the same for every part. Nothing has to cross between parts.
Inputs may be any that keep to these rules, and one draw needn't show every extreme that they name: `routes`: each row names 4 different numbers. In each aligned block of 8 rows (the rows of one device) no number is named by more than 4 rows.
All inputs are finite; a program needn't handle non-finite values.
Results may differ from a plain program's by a relative error of at most 0.006.
Values may be sent and summed in bfloat16 or wider, within the bound.
A program may use at most 192 MiB of HBM per device.

v0:
```python
import jax
import jax.numpy as jnp
from jax import lax
from jax.sharding import PartitionSpec as P

EXPERTS = 8
CAP = 4


def route_table(routes, route_weights):
    experts_iota = jnp.arange(EXPERTS, dtype=jnp.int32)
    matched = routes[:, :, None] == experts_iota[None, None, :]
    weight_table = jnp.sum(
        jnp.where(matched, route_weights.astype(jnp.float32)[:, :, None], jnp.float32(0.0)), axis=1
    )
    return (jnp.any(matched, axis=1), weight_table)


def slot_matrix(chosen, capacity):
    rank_table = jnp.cumsum(chosen.astype(jnp.int32), axis=-1) - 1
    slot_iota = jnp.arange(capacity, dtype=jnp.int32)
    onehot = chosen[..., None, :] & (rank_table[..., None, :] == slot_iota[:, None])
    return onehot.astype(jnp.float32)


def slot_rank(chosen, capacity):
    rank_table = jnp.cumsum(chosen.astype(jnp.int32), axis=-1) - 1
    return jnp.clip(rank_table, 0, capacity - 1)


def expert_math(row_tokens, row_cots, coefficient, gate_rows, up_rows, down_rows):
    contract_last = (((1,), (1,)), ((), ()))
    contract_first = (((0,), (0,)), ((), ()))
    gate_pre = lax.dot_general(
        row_tokens, gate_rows, contract_last, preferred_element_type=jnp.float32
    )
    up_pre = lax.dot_general(row_tokens, up_rows, contract_last, preferred_element_type=jnp.float32)
    sigmoid_gate = jax.nn.sigmoid(gate_pre)
    activated = gate_pre * sigmoid_gate
    hidden = (activated * up_pre).astype(jnp.bfloat16)
    out_grad = (coefficient[:, None] * row_cots.astype(jnp.float32)).astype(jnp.bfloat16)
    hidden_grad = lax.dot_general(
        out_grad, down_rows, contract_last, preferred_element_type=jnp.float32
    )
    grad_down = lax.dot_general(
        hidden, out_grad, contract_first, preferred_element_type=jnp.float32
    ).astype(jnp.bfloat16)
    up_grad = (hidden_grad * activated).astype(jnp.bfloat16)
    gate_grad = (
        hidden_grad * up_pre * sigmoid_gate * (1.0 + gate_pre * (1.0 - sigmoid_gate))
    ).astype(jnp.bfloat16)
    grad_up = lax.dot_general(
        up_grad, row_tokens, contract_first, preferred_element_type=jnp.float32
    ).astype(jnp.bfloat16)
    grad_gate = lax.dot_general(
        gate_grad, row_tokens, contract_first, preferred_element_type=jnp.float32
    ).astype(jnp.bfloat16)
    row_grads = jnp.dot(gate_grad, gate_rows, preferred_element_type=jnp.float32) + jnp.dot(
        up_grad, up_rows, preferred_element_type=jnp.float32
    )
    return ((grad_gate, grad_up, grad_down), row_grads)


def body(tokens, cotangent, routes, route_weights, w_gate, w_up, w_down):
    cycle_size = lax.axis_size("ep")
    group_size = cycle_size // EXPERTS
    device_place = lax.axis_index("ep")
    expert_index = device_place // group_size
    local_rows, model_width = tokens.shape
    capacity = CAP
    slot_rows = cycle_size * capacity
    chosen, weight_table = route_table(routes, route_weights)
    all_tokens, all_cots, all_weights = (
        lax.all_gather(tokens, "ep", axis=0, tiled=True),
        lax.all_gather(cotangent, "ep", axis=0, tiled=True),
        lax.all_gather(weight_table.astype(jnp.bfloat16), "ep", axis=0, tiled=True),
    )
    column = (
        lax.dynamic_slice_in_dim(all_weights, expert_index, 1, 1)[:, 0]
        .astype(jnp.float32)
        .reshape(cycle_size, local_rows)
    )
    picked = column > 0.0
    block_slots = slot_matrix(picked, capacity)
    block_onehot = block_slots.astype(jnp.bfloat16)
    row_tokens = (
        jnp.einsum(
            "scj,sjd->scd",
            block_onehot,
            all_tokens.reshape(cycle_size, local_rows, model_width),
            preferred_element_type=jnp.float32,
        )
        .astype(jnp.bfloat16)
        .reshape(slot_rows, model_width)
    )
    row_cots = (
        jnp.einsum(
            "scj,sjd->scd",
            block_onehot,
            all_cots.reshape(cycle_size, local_rows, model_width),
            preferred_element_type=jnp.float32,
        )
        .astype(jnp.bfloat16)
        .reshape(slot_rows, model_width)
    )
    coefficient = jnp.sum(block_slots * column[:, None, :], axis=2).reshape(slot_rows)
    gradients, row_grads = expert_math(row_tokens, row_cots, coefficient, w_gate, w_up, w_down)
    block_rank = slot_rank(picked, capacity)
    looked_up = jnp.take_along_axis(
        row_grads.reshape(cycle_size, capacity, model_width), block_rank[:, :, None], axis=1
    )
    per_token = jnp.where(picked[:, :, None], looked_up, jnp.float32(0.0)).reshape(
        cycle_size * local_rows, model_width
    )
    token_grads = lax.psum_scatter(per_token, "ep", scatter_dimension=0, tiled=True)
    return (token_grads.astype(jnp.bfloat16), gradients[0], gradients[1], gradients[2])


def solution(mesh):
    placed = (
        P(("groups", "ep"), None),
        P(("groups", "ep"), None),
        P(("groups", "ep"), None),
        P(("groups", "ep"), None),
        P("ep", None),
        P("ep", None),
        P("ep", None),
    )
    return jax.shard_map(
        body,
        mesh=mesh,
        in_specs=placed,
        out_specs=(
            P(("groups", "ep"), None),
            P(("groups", "ep"), None),
            P(("groups", "ep"), None),
            P(("groups", "ep"), None),
        ),
        check_vma=False,
    )
```

profile of v0, /device:TPU:0, one launch (start us, length us, event | category | flops | bytes accessed | tf_op | source)
XLA Modules:
  0.0 200.1 jit_solution(17749898755902725246)
XLA Ops:
  7.2 0.0 reduce-scatter.2.cloned.1.call-start
  7.2 0.7 convert_element_type.73
  7.9 0.8 select_reduce_fusion.1
  8.7 23.2 %all_gather.9 = bf16[128,8]{1,0:T(8,128)(2,1)S(1)} all-gather(bf16[8,8]{1,0:T(8,128)(2,1)S(1)} %select_reduce_fusion.1), channel_id=1, replica_groups=mesh['groups'=2,'ep'=16] {'ep'}, dimensions={0}, use_global_device_ids=true | all-gather | bytes 2176 | tf_op jit(solution)/shard_map/all_gather | solution.py:76
  31.8 0.2 convert_reduce_fusion
  32.0 0.2 fusion.5
  32.2 0.1 reshape.98
  32.3 0.2 reduce_window_sum.12
  32.5 0.1 min.16
  32.6 0.1 copy.27
  32.6 0.1 select_reduce_fusion
  32.8 0.1 mul.41
  32.9 0.1 copy.28
  32.9 0.1 reshape.100
  33.0 19.8 %all_gather.11 = bf16[128,3072]{1,0:T(8,128)(2,1)S(1)} all-gather(bf16[8,3072]{1,0:T(8,128)(2,1)} %param.7), channel_id=1, replica_groups=mesh['groups'=2,'ep'=16] {'ep'}, dimensions={0}, use_global_device_ids=true | all-gather | bytes 835584 | tf_op jit(solution)/shard_map/all_gather | solution.py:74
  52.9 0.4 convolution_convert_fusion.3
  53.2 0.1 reshape.96
  53.3 0.0 copy-start.3
  53.3 10.8 %fusion.16 = f32[64,2688]{1,0:T(8,128)S(1)} fusion(bf16[64,3072]{1,0:T(8,128)(2,1)S(1)} %reshape.96, bf16[2688,3072]{1,0:T(8,128)(2,1)} %param.11), kind=kOutput, calls=%fused_computation.39 | convolution fusion | flops 1056964608 | bytes 17596416 | tf_op jit(solution)/shard_map/dot_general | solution.py:34
  64.1 10.8 %fusion.15 = f32[64,2688]{1,0:T(8,128)S(1)} fusion(bf16[64,3072]{1,0:T(8,128)(2,1)S(1)} %reshape.96, bf16[2688,3072]{1,0:T(8,128)(2,1)} %param.12), kind=kOutput, calls=%fused_computation.38 | convolution fusion | flops 1056964608 | bytes 17596416 | tf_op jit(solution)/shard_map/dot_general | solution.py:37
  74.9 0.0 copy-done.3
  74.9 21.3 %all_gather.10 = bf16[128,3072]{1,0:T(8,128)(2,1)S(1)} all-gather(bf16[8,3072]{1,0:T(8,128)(2,1)S(1)} %copy-done.3), channel_id=1, replica_groups=mesh['groups'=2,'ep'=16] {'ep'}, dimensions={0}, use_global_device_ids=true | all-gather | bytes 835584 | tf_op jit(solution)/shard_map/all_gather | solution.py:75
  96.2 0.3 fusion
  96.5 0.3 reshape.99
  96.8 10.8 %multiply_convert_fusion.2 = (bf16[64,2688]{1,0:T(8,128)(2,1)S(1)}, bf16[64,2688]{1,0:T(8,128)(2,1)S(1)}) fusion(f32[64,2688]{1,0:T(8,128)S(1)} %fusion.16, f32[64,2688]{1,0:T(8,128)S(1)} %fusion.15, bf16[2688,3072]{1,0:T(8,128)(2,1)} %param.13, f32[64,3072]{1,0:T(8,128)S(1)} %reshape.99, f32[64]{0:T(128)S(1)} %mul.41), kind=kOutput, calls=%fused_computation.13 | convolution fusion | flops 1059594240 | bytes 19366144 | tf_op jit(solution)/shard_map/dot_general | solution.py:42
  107.6 0.0 copy-start
  107.7 0.0 copy-start.2
  107.7 9.0 %fusion.17 = f32[64,3072]{1,0:T(8,128)S(1)} fusion(bf16[64,2688]{1,0:T(8,128)(2,1)S(1)} %get-tuple-element.7, bf16[2688,3072]{1,0:T(8,128)(2,1)} %param.11), kind=kOutput, calls=%fused_computation.40 | convolution fusion | flops 1056964608 | bytes 17645568 | tf_op jit(solution)/shard_map/dot_general | solution.py:58
  116.7 0.0 copy-done
  116.7 0.0 copy-done.2
  116.7 9.7 %convolution_add_fusion = f32[64,3072]{1,0:T(8,128)} fusion(f32[64,3072]{1,0:T(8,128)S(1)} %fusion.17, bf16[64,2688]{1,0:T(8,128)(2,1)S(1)} %get-tuple-element.6, bf16[2688,3072]{1,0:T(8,128)(2,1)} %param.12), kind=kOutput, calls=%fused_computation.4 | convolution fusion | flops 1057161216 | bytes 18432000 | tf_op jit(solution)/shard_map/dot_general | solution.py:58
  126.4 1.4 reshape.97
  127.7 4.1 %gather_fusion = f32[128,3072]{1,0:T(8,128)} fusion(f32[16,4,3072]{2,1,0:T(4,128)S(1)} %reshape.97, s32[128]{0:T(128)S(1)} %reshape.100), kind=kCustom, calls=%fused_computation | custom fusion | bytes 3146752 | tf_op jit(solution)/shard_map/jit(take_along_axis)/gather | solution.py:109
  131.9 0.0 copy-start.1
  131.9 2.9 %select_select_fusion = f32[128,3072]{1,0:T(8,128)} fusion(f32[128,3072]{1,0:T(8,128)} %gather_fusion, pred[128]{0:T(512)(128)(4,1)S(1)} %compare_and_fusion, pred[128]{0:T(512)(128)(4,1)S(1)} %fusion.5), kind=kLoop, calls=%fused_computation.8 | loop fusion | flops 786432 | bytes 3145984 | tf_op jit(solution)/shard_map/jit(_where)/select_n | solution.py:112
  134.8 0.0 reduce-scatter.2.cloned.1.call-update
  134.8 9.6 %convolution_convert_fusion.1 = bf16[2688,3072]{1,0:T(8,128)(2,1)} fusion(bf16[64,2688]{1,0:T(8,128)(2,1)} %copy-done.2, bf16[64,3072]{1,0:T(8,128)(2,1)S(1)} %reshape.96), kind=kOutput, calls=%fused_computation.2 | convolution fusion | flops 1065222144 | bytes 17252352 | tf_op jit(solution)/shard_map/dot_general | solution.py:52
  144.4 0.0 copy-done.1
  144.4 8.4 %convolution_convert_fusion.2 = bf16[2688,3072]{1,0:T(8,128)(2,1)} fusion(bf16[64,2688]{1,0:T(8,128)(2,1)S(1)} %copy-done.1, bf16[64,3072]{1,0:T(8,128)(2,1)S(1)} %reshape.96), kind=kOutput, calls=%fused_computation.3 | convolution fusion | flops 1065222144 | bytes 17252352 | tf_op jit(solution)/shard_map/dot_general | solution.py:55
  152.8 8.4 %convolution_convert_fusion = bf16[2688,3072]{1,0:T(8,128)(2,1)} fusion(f32[64,2688]{1,0:T(8,128)S(1)} %fusion.15, f32[64,2688]{1,0:T(8,128)S(1)} %fusion.16, f32[64,3072]{1,0:T(8,128)S(1)} %reshape.99, f32[64]{0:T(128)S(1)} %mul.41), kind=kOutput, calls=%fused_computation.1 | convolution fusion | flops 1066647552 | bytes 18678016 | tf_op jit(solution)/shard_map/dot_general | solution.py:45
  161.2 30.5 %reduce-scatter.2.cloned.1.call-done = f32[8,3072]{1,0:T(8,128)} async-done(((f32[128,3072]{1,0:T(8,128)}), f32[8,3072]{1,0:T(8,128)}) %reduce-scatter.2.cloned.1.call-update) | async-done | bytes 98320 | tf_op jit(solution)/shard_map/reduce_scatter | solution.py:115
  191.7 1.5 convert_element_type.88
  (4 shorter events, 0.0 us)
Async XLA Ops:
  7.2 184.6 %reduce-scatter.2.cloned.1.call-start = ((), (), s32[]{:S(2)}) async-start(), calls=%async_computation.1 | async-start | bytes 1671168 | tf_op jit(solution)/shard_map/reduce_scatter | solution.py:115
  53.3 21.6 %copy-start.3 = (bf16[8,3072]{1,0:T(8,128)(2,1)S(1)}, bf16[8,3072]{1,0:T(8,128)(2,1)}, u32[]{:S(2)}) copy-start(bf16[8,3072]{1,0:T(8,128)(2,1)} %param.8) | copy-start | bytes 147460
  107.6 9.0 %copy-start = (bf16[64,2688]{1,0:T(8,128)(2,1)}, bf16[64,2688]{1,0:T(8,128)(2,1)S(1)}, u32[]{:S(2)}) copy-start(bf16[64,2688]{1,0:T(8,128)(2,1)S(1)} %get-tuple-element.7) | copy-start | bytes 1032196
  107.7 9.0 %copy-start.2 = (bf16[64,2688]{1,0:T(8,128)(2,1)}, bf16[64,2688]{1,0:T(8,128)(2,1)S(1)}, u32[]{:S(2)}) copy-start(bf16[64,2688]{1,0:T(8,128)(2,1)S(1)} %get-tuple-element.6) | copy-start | bytes 1032196
  131.9 12.5 %copy-start.1 = (bf16[64,2688]{1,0:T(8,128)(2,1)S(1)}, bf16[64,2688]{1,0:T(8,128)(2,1)}, u32[]{:S(2)}) copy-start(bf16[64,2688]{1,0:T(8,128)(2,1)} %copy-done) | copy-start | bytes 1032196
Sparse Core Ops, SparseCore 0:
  134.9 56.7 reduce-scatter.1
where the time goes:
time: 201 us; the launch traced here: 200 us
  matrix products  78.2 us (39%)
  blocking collectives  64.3 us (32%)
  waiting for transfers between devices  30.5 us (15%)
  between operations  14.2 us (7%)
  other arithmetic  6.49 us (3%)
  local copies, waits for them, and re-layouts  6.36 us (3%)
    reduce_scatter x1, waiting for transfers between devices, body(): lax.psum_scatter(per_token, 'ep', scatter_dimension=0, tiled=True)  30.5 us
    all_gather x1, blocking collectives, body(): lax.all_gather(weight_table.astype(jnp.bfloat16), 'ep', axis=0, tiled=True)  23.2 us
    all_gather x1, blocking collectives, body(): lax.all_gather(cotangent, 'ep', axis=0, tiled=True)  21.3 us
    all_gather x1, blocking collectives, body(): lax.all_gather(tokens, 'ep', axis=0, tiled=True)  19.8 us
    dot_general x1, matrix products, expert_math(): lax.dot_general(out_grad, down_rows, contract_last, preferred_element_typ...  10.8 us
    dot_general x1, matrix products, expert_math(): lax.dot_general(row_tokens, gate_rows, contract_last, preferred_element_t...  10.8 us
    dot_general x1, matrix products, expert_math(): lax.dot_general(row_tokens, up_rows, contract_last, preferred_element_typ...  10.8 us
    dot_general x1, matrix products, expert_math(): jnp.dot(up_grad, up_rows, preferred_element_type=jnp.float32)  9.66 us
  transfers between devices with their start and end apart: 1, of which 1 were waited for; matrix products, arithmetic and copies ran while one was open for 13% of the time, Pallas kernels for 0%

commit v1 on v0

--- a/solution.py
+++ b/solution.py
@@ -1,10 +1,316 @@
+import functools
 import jax
 import jax.numpy as jnp
 from jax import lax
+from jax.experimental import pallas as pl
+from jax.experimental.pallas import tpu as pltpu
 from jax.sharding import PartitionSpec as P
 
 EXPERTS = 8
 CAP = 4
+LANES = 128
+CHUNK = 384
+NCOL = 256
+OUT_ROWS = 384
+MESH = pl.DeviceIdType.MESH
+F32 = jnp.float32
+BF16 = jnp.bfloat16
+
+
+def gather_blocks(blocks, send_sem, recv_sem):
+    me = lax.axis_index("ep")
+    z, y, c = me // 4, (me // 2) % 2, me % 2
+
+    def place(zz, yy, cc):
+        return (zz * 2 + yy) * 2 + cc
+
+    up, down = place(z + 1, y, c), place(z - 1, y, c)
+    across, sibling = place(z, 1 - y, c), place(z, y, 1 - c)
+
+    def copy(kind, slot, target):
+        return pltpu.make_async_remote_copy(
+            src_ref=blocks.at[slot],
+            dst_ref=blocks.at[slot],
+            send_sem=send_sem.at[kind, slot],
+            recv_sem=recv_sem.at[slot],
+            device_id={"ep": target},
+            device_id_type=MESH,
+        )
+
+    def landed(slot):
+        copy(0, slot, sibling).wait_recv()
+
+    def relay_from_below(slot):
+        @pl.when(z < 3)
+        def _():
+            copy(1, slot, up).start()
+
+    def relay_from_above(slot):
+        @pl.when(z > 0)
+        def _():
+            copy(2, slot, down).start()
+
+    def spread(slot):
+        copy(3, slot, across).start()
+        copy(0, slot, sibling).start()
+
+    def crossed(zz):
+        slot = place(zz, 1 - y, c)
+        landed(slot)
+        copy(0, slot, sibling).start()
+
+    relay_from_below(me)
+    relay_from_above(me)
+    spread(me)
+    for d in (1, 2, 3):
+
+        @pl.when(z >= d)
+        def _():
+            slot = place(z - d, y, c)
+            landed(slot)
+            relay_from_below(slot)
+            spread(slot)
+
+        @pl.when(z + d <= 3)
+        def _():
+            slot = place(z + d, y, c)
+            landed(slot)
+            relay_from_above(slot)
+            spread(slot)
+
+        if d == 1:
+            crossed(z)
+        else:
+
+            @pl.when(z >= d - 1)
+            def _():
+                crossed(z - (d - 1))
+
+            @pl.when(z + d - 1 <= 3)
+            def _():
+                crossed(z + d - 1)
+
+    @pl.when(z >= 3)
+    def _():
+        crossed(z - 3)
+
+    @pl.when(z <= 0)
+    def _():
+        crossed(z + 3)
+
+    for zz in range(4):
+        for yy in range(2):
+            landed(place(zz, yy, 1 - c))
+
+    def drain():
+        for zz in range(4):
+            slot = place(zz, y, c)
+
+            @pl.when((zz <= z) & (z < 3))
+            def _():
+                copy(1, slot, up).wait_send()
+
+            @pl.when((zz >= z) & (z > 0))
+            def _():
+                copy(2, slot, down).wait_send()
+
+            copy(3, slot, across).wait_send()
+            copy(0, slot, sibling).wait_send()
+            copy(0, place(zz, 1 - y, c), sibling).wait_send()
+
+    return drain
+
+
+def greet():
+    me = lax.axis_index("ep")
+    z = me // 4
+    barrier = pltpu.get_barrier_semaphore()
+
+    def hello(other):
+        pl.semaphore_signal(barrier, inc=1, device_id={"ep": other}, device_id_type=MESH)
+
+    hello(me + 1 - 2 * (me % 2))
+    hello(me + 2 - 4 * ((me // 2) % 2))
+
+    @pl.when(z > 0)
+    def _():
+        hello(me - 4)
+
+    @pl.when(z < 3)
+    def _():
+        hello(me + 4)
+
+    @pl.when((z > 0) & (z < 3))
+    def _():
+        pl.semaphore_wait(barrier, 4)
+
+    @pl.when((z <= 0) | (z >= 3))
+    def _():
+        pl.semaphore_wait(barrier, 3)
+
+
+def forward_kernel(
+    tok_ref, cot_ref, routes_ref, rw_ref, wg_hbm, wu_hbm, wd_hbm,
+    gu_ref, hid_ref, x_ref, og_ref, part_ref,
+    w2, wd, blocks, xt, ogt, gut, wsem, send_sem, recv_sem,
+):
+    me = lax.axis_index("ep")
+    expert = me // (lax.axis_size("ep") // EXPERTS)
+    rows, width = tok_ref.shape
+    hidden = wd.shape[0]
+    parts = hidden // CHUNK
+    n = blocks.shape[0]
+
+    def weight_copies(i):
+        at = pl.multiple_of(i * CHUNK, CHUNK)
+        src = pl.ds(at, CHUNK)
+        two = pl.multiple_of(i * 2 * CHUNK, CHUNK)
+        return (
+            pltpu.make_async_copy(wg_hbm.at[src], w2.at[pl.ds(two, CHUNK)], wsem.at[0, i]),
+            pltpu.make_async_copy(wu_hbm.at[src], w2.at[pl.ds(two + CHUNK, CHUNK)], wsem.at[1, i]),
+            pltpu.make_async_copy(wd_hbm.at[src], wd.at[src], wsem.at[2, i]),
+        )
+
+    for i in range(parts):
+        for one in weight_copies(i):
+            one.start()
+    greet()
+
+    lane = lax.broadcasted_iota(jnp.int32, (rows, LANES), 1)
+    table = jnp.zeros((rows, LANES), F32)
+    for k in range(routes_ref.shape[1]):
+        table += jnp.where(lane == routes_ref[:, k : k + 1], rw_ref[:, k : k + 1].astype(F32), 0.0)
+    own = jnp.concatenate([tok_ref[...].astype(F32), cot_ref[...].astype(F32)], axis=0)
+    blocks[me, :, :width] = own.astype(BF16)
+    blocks[me, :, width:] = jnp.concatenate([table, table], axis=0).astype(BF16)
+
+    drain = gather_blocks(blocks, send_sem, recv_sem)
+
+    for pair in range(n // 2):
+        toks, ogs = [], []
+        for b in (2 * pair, 2 * pair + 1):
+            block = blocks[b].astype(F32)
+            toks.append(block[:rows, :width])
+            coef = jnp.sum(
+                jnp.where(lane == expert, block[rows:, width:], 0.0), axis=1, keepdims=True
+            )
+            ogs.append(coef * block[rows:, :width])
+        at = slice(2 * rows * pair, 2 * rows * (pair + 1))
+        x_ref[at, :] = jnp.concatenate(toks, axis=0).astype(BF16)
+        og_ref[at, :] = jnp.concatenate(ogs, axis=0).astype(BF16)
+    for j in range(0, width, 512):
+        xt[j : j + 512, :] = x_ref[:, j : j + 512].T
+        ogt[j : j + 512, :] = og_ref[:, j : j + 512].T
+
+    def forward(i, carry):
+        for one in weight_copies(i):
+            one.wait()
+        at = pl.ds(pl.multiple_of(i * CHUNK, CHUNK), CHUNK)
+        low = pl.multiple_of(i * 2 * CHUNK, CHUNK)
+        both = jnp.dot(w2[pl.ds(low, 2 * CHUNK), :], xt[...], preferred_element_type=F32)
+        gate, up = both[:CHUNK], both[CHUNK:]
+        hgrad = jnp.dot(wd[at, :], ogt[...], preferred_element_type=F32)
+        sig = 1.0 / (1.0 + jnp.exp(-gate))
+        act = gate * sig
+        hid_ref[at, :] = (act * up).astype(BF16)
+        up_grad = (hgrad * act).astype(BF16)
+        gate_grad = (hgrad * up * sig * (1.0 + gate * (1.0 - sig))).astype(BF16)
+        gu_ref[pl.ds(low, CHUNK), :] = gate_grad
+        gu_ref[pl.ds(low + CHUNK, CHUNK), :] = up_grad
+        gut[:, pl.ds(low, CHUNK)] = gate_grad.T
+        gut[:, pl.ds(low + CHUNK, CHUNK)] = up_grad.T
+        return carry
+
+    lax.fori_loop(0, parts, forward, 0)
+
+    def back(j, carry):
+        cols = pl.ds(pl.multiple_of(j * NCOL, NCOL), NCOL)
+        part_ref[:, cols] = jnp.dot(gut[...], w2[:, cols], preferred_element_type=F32)
+        return carry
+
+    lax.fori_loop(0, width // NCOL, back, 0)
+    drain()
+
+
+def outer_kernel(gu_ref, hid_ref, x_ref, og_ref, gate_out, up_out, down_out):
+    half = gate_out.shape[0]
+    both = jnp.dot(gu_ref[...], x_ref[...], preferred_element_type=F32).astype(BF16)
+    gate_out[...] = both[:half]
+    up_out[...] = both[half:]
+    down_out[...] = jnp.dot(hid_ref[...], og_ref[...], preferred_element_type=F32).astype(BF16)
+
+
+def forward_call(tokens, cotangent, routes, route_weights, w_gate, w_up, w_down):
+    n = lax.axis_size("ep")
+    rows, width = tokens.shape
+    hidden = w_gate.shape[0]
+    total = n * rows
+    parts = hidden // CHUNK
+    vmem = pl.BlockSpec(memory_space=pltpu.VMEM)
+    hbm = pl.BlockSpec(memory_space=pl.ANY)
+    return pl.pallas_call(
+        forward_kernel,
+        out_shape=(
+            jax.ShapeDtypeStruct((2 * hidden, total), BF16),
+            jax.ShapeDtypeStruct((hidden, total), BF16),
+            jax.ShapeDtypeStruct((total, width), BF16),
+            jax.ShapeDtypeStruct((total, width), BF16),
+            jax.ShapeDtypeStruct((total, width), F32),
+        ),
+        in_specs=[vmem] * 4 + [hbm] * 3,
+        out_specs=(vmem,) * 5,
+        scratch_shapes=[
+            pltpu.VMEM((2 * hidden, width), BF16),
+            pltpu.VMEM((hidden, width), BF16),
+            pltpu.VMEM((n, 2 * rows, width + LANES), BF16),
+            pltpu.VMEM((width, total), BF16),
+            pltpu.VMEM((width, total), BF16),
+            pltpu.VMEM((total, 2 * hidden), BF16),
+            pltpu.SemaphoreType.DMA((3, parts)),
+            pltpu.SemaphoreType.DMA((4, n)),
+            pltpu.SemaphoreType.DMA((n,)),
+        ],
+        compiler_params=pltpu.CompilerParams(
+            collective_id=0, has_side_effects=True, vmem_limit_bytes=63 * 1024 * 1024
+        ),
+        name="gather_forward",
+    )(tokens, cotangent, routes, route_weights, w_gate, w_up, w_down)
+
+
+def outer_call(gu, hid, x, og):
+    hidden, total = hid.shape
+    width = x.shape[1]
+    whole = pl.BlockSpec((total, width), lambda i: (0, 0))
+    out = pl.BlockSpec((OUT_ROWS, width), lambda i: (i, 0))
+    shape = jax.ShapeDtypeStruct((hidden, width), BF16)
+    return pl.pallas_call(
+        outer_kernel,
+        grid=(hidden // OUT_ROWS,),
+        out_shape=(shape,) * 3,
+        in_specs=[
+            pl.BlockSpec((2 * OUT_ROWS, total), lambda i: (i, 0)),
+            pl.BlockSpec((OUT_ROWS, total), lambda i: (i, 0)),
+            whole,
+            whole,
+        ],
+        out_specs=(out,) * 3,
+        compiler_params=pltpu.CompilerParams(vmem_limit_bytes=48 * 1024 * 1024),
+        cost_estimate=pl.CostEstimate(
+            flops=6 * hidden * total * width,
+            bytes_accessed=6 * hidden * width + 4 * total * width,
+            transcendentals=0,
+        ),
+        name="weight_grads",
+    )(gu, hid, x, og)
+
+
+def fused_body(tokens, cotangent, routes, route_weights, w_gate, w_up, w_down):
+    gu, hid, x, og, partial_grads = forward_call(
+        tokens, cotangent, routes, route_weights, w_gate, w_up, w_down
+    )
+    token_grads = lax.psum_scatter(partial_grads, "ep", scatter_dimension=0, tiled=True)
+    grad_gate, grad_up, grad_down = outer_call(gu, hid, x, og)
+    return token_grads.astype(BF16), grad_gate, grad_up, grad_down
 
 
 def route_table(routes, route_weights):
@@ -127,7 +433,7 @@
         P("ep", None),
     )
     return jax.shard_map(
-        body,
+        fused_body if mesh.shape["ep"] == 16 else body,
         mesh=mesh,
         in_specs=placed,
         out_specs=(

time: 201 us -> 123 us (0.61)
  matrix products: 78.2 us -> 0 us
  blocking collectives: 64.3 us -> 0 us
  Pallas kernels: 0 us -> 64.1 us
  other arithmetic: 6.49 us -> 1.52 us
  waiting for transfers between devices: 30.5 us -> 35.2 us
    dot_general x10 -> x0, matrix products: 78.2 us -> none  [the longest x1 10.8 us: expert_math(): lax.dot_general(out_grad, down_rows, contract_last, preferred_element_typ...]
    all_gather x3 -> x0, blocking collectives: 64.3 us -> none  [the longest x1 23.2 us: body(): lax.all_gather(weight_table.astype(jnp.bfloat16), 'ep', axis=0, tiled=True)]
    pallas_call x0 -> x2, Pallas kernels: none -> 64.1 us  [the longest x1 45.6 us: forward_call(): pl.pallas_call(forward_kernel, out_shape=(jax.ShapeDtypeStruct((2 * hidde...]
    unnamed x8 -> x10, local copies, waits for them, and re-layouts: 0.02 us -> 7.39 us
    reduce_scatter x1, waiting for transfers between devices: 30.5 us -> 35.2 us  [fused_body(): lax.psum_scatter(partial_grads, 'ep', scatter_dimension=0, tiled=True)]
    gather x3 -> x0, local copies, waits for them, and re-layouts: 4.3 us -> none  [body(): jnp.take_along_axis(row_grads.reshape(cycle_size, capacity, model_width),...]
    select_n x1 -> x0, other arithmetic: 2.88 us -> none  [body(): jnp.where(picked[:, :, None], looked_up, jnp.float32(0.0))]
  transfers between devices with their start and end apart: 1 -> 1, of which waited for: 1 -> 1; matrix products, arithmetic and copies ran while one was open for 13% -> 0% of each run, Pallas kernels for 0% -> 15%
where the time goes in v1:
time: 123 us; the launch traced here: 122 us
  Pallas kernels  64.1 us (52%)
  waiting for transfers between devices  35.2 us (29%)
  between operations  14 us (11%)
  local copies, waits for them, and re-layouts  7.39 us (6%)
  other arithmetic  1.52 us (1%)
    pallas_call x1, Pallas kernels, forward_call(): pl.pallas_call(forward_kernel, out_shape=(jax.ShapeDtypeStruct((2 * hidde...  45.6 us
    reduce_scatter x1, waiting for transfers between devices, fused_body(): lax.psum_scatter(partial_grads, 'ep', scatter_dimension=0, tiled=True)  35.2 us
    pallas_call x1, Pallas kernels, outer_call(): pl.pallas_call(outer_kernel, grid=(hidden // OUT_ROWS,), out_shape=(shape...  18.5 us
    unnamed x10, local copies, waits for them, and re-layouts  7.39 us
  transfers between devices with their start and end apart: 1, of which 1 were waited for; matrix products, arithmetic and copies ran while one was open for 0% of the time, Pallas kernels for 15%

profile of v1, /device:TPU:0, one launch (start us, length us, event | category | flops | bytes accessed | tf_op | source)
XLA Modules:
  0.0 122.3 jit_solution(6184362621597141261)
XLA Ops:
  7.2 0.0 reduce-scatter.2.cloned.1.call-start
  7.2 1.3 %copy.12.rw_ref = bf16[8,4]{1,0:T(8,128)(2,1)} copy(bf16[8,4]{0,1:T(4,128)(2,1)} %param.10) | data formatting | bytes 128 | tf_op args[3]
  8.6 1.3 %copy.11.routes_ref = s32[8,4]{1,0:T(8,128)} copy(s32[8,4]{0,1:T(4,128)} %param.9) | data formatting | bytes 256 | tf_op args[2]
  9.9 45.6 %gather_forward.1 = (bf16[5376,128]{1,0:T(8,128)(2,1)}, bf16[2688,128]{1,0:T(8,128)(2,1)}, bf16[128,3072]{1,0:T(8,128)(2,1)}, bf16[128,3072]{1,0:T(8,128)(2,1)}, f32[128,3072]{1,0:T(8,128)}) custom-call(bf16[8,3072]{1,0:T(8,128)(2,1)} %tok_ref.1, bf16[8,3072]{1,0:T(8,128)(2,1)} %cot_ref.1, s32[8,4]{1,0:T(8,128)} %copy.11.routes_ref, ...), custom_call_target="tpu_custom_call" | custom-call | tf_op jit(solution)/shard_map/gather_forward/pallas_call | solution.py:251
  55.5 0.0 reduce-scatter.2.cloned.1.call-update
  55.5 0.0 copy-start
  55.5 1.3 %copy-done = bf16[5376,128]{1,0:T(8,128)(2,1)S(1)} copy-done((bf16[5376,128]{1,0:T(8,128)(2,1)S(1)}, bf16[5376,128]{1,0:T(8,128)(2,1)}, u32[]{:S(2)}) %copy-start) | copy-done | bytes 1376280
  56.9 0.0 copy-start.1
  56.9 1.1 copy-done.1
  58.0 0.0 copy-start.2
  58.0 1.1 copy-done.2
  59.1 0.0 copy-start.3
  59.1 1.1 copy-done.3
  60.2 18.5 %weight_grads.1 = (bf16[2688,3072]{1,0:T(8,128)(2,1)}, bf16[2688,3072]{1,0:T(8,128)(2,1)}, bf16[2688,3072]{1,0:T(8,128)(2,1)}) custom-call(bf16[5376,128]{1,0:T(8,128)(2,1)S(1)} %copy-done, bf16[2688,128]{1,0:T(8,128)(2,1)S(1)} %copy-done.3, bf16[128,3072]{1,0:T(8,128)(2,1)S(1)} %copy-done.1, bf16[128,3072]{1,0:T(8,128)(2,1)S(1)} %copy-done.2), custom_call_target="tpu_custom_call" | custom-call | flops 6341787648 | bytes 51118080 | tf_op jit(solution)/shard_map/weight_grads/pallas_call | solution.py:286
  78.8 35.2 %reduce-scatter.2.cloned.1.call-done = f32[8,3072]{1,0:T(8,128)} async-done(((f32[128,3072]{1,0:T(8,128)}), f32[8,3072]{1,0:T(8,128)}) %reduce-scatter.2.cloned.1.call-update) | async-done | bytes 98320 | tf_op jit(solution)/shard_map/reduce_scatter | solution.py:311
  114.0 1.5 %convert_element_type.3 = bf16[8,3072]{1,0:T(8,128)(2,1)} convert(f32[8,3072]{1,0:T(8,128)} %reduce-scatter.2.cloned.1.call-done) | non-fusion elementwise | flops 24576 | bytes 147456 | tf_op jit(solution)/shard_map/convert_element_type | solution.py:313
Async XLA Ops:
  7.2 106.8 %reduce-scatter.2.cloned.1.call-start = ((), (), s32[]{:S(2)}) async-start(), calls=%async_computation.1 | async-start | bytes 1671168 | tf_op jit(solution)/shard_map/reduce_scatter | solution.py:311
  55.5 1.3 %copy-start = (bf16[5376,128]{1,0:T(8,128)(2,1)S(1)}, bf16[5376,128]{1,0:T(8,128)(2,1)}, u32[]{:S(2)}) copy-start(bf16[5376,128]{1,0:T(8,128)(2,1)} %get-tuple-element.13.gu_ref) | copy-start | bytes 4128772
  56.9 1.1 copy-start.1
  58.0 1.1 copy-start.2
  59.1 1.1 copy-start.3
Sparse Core Ops, SparseCore 0:
  55.6 58.2 reduce-scatter.1

commit v2 on v1

--- a/solution.py
+++ b/solution.py
@@ -10,7 +10,7 @@
 CAP = 4
 LANES = 128
 CHUNK = 384
-NCOL = 256
+HALF = 512
 OUT_ROWS = 384
 MESH = pl.DeviceIdType.MESH
 F32 = jnp.float32
@@ -121,38 +121,21 @@
     return drain
 
 
-def greet():
+def greet(n):
     me = lax.axis_index("ep")
-    z = me // 4
     barrier = pltpu.get_barrier_semaphore()
-
-    def hello(other):
-        pl.semaphore_signal(barrier, inc=1, device_id={"ep": other}, device_id_type=MESH)
-
-    hello(me + 1 - 2 * (me % 2))
-    hello(me + 2 - 4 * ((me // 2) % 2))
-
-    @pl.when(z > 0)
-    def _():
-        hello(me - 4)
-
-    @pl.when(z < 3)
-    def _():
-        hello(me + 4)
-
-    @pl.when((z > 0) & (z < 3))
-    def _():
-        pl.semaphore_wait(barrier, 4)
-
-    @pl.when((z <= 0) | (z >= 3))
-    def _():
-        pl.semaphore_wait(barrier, 3)
+    for k in range(1, n):
+        pl.semaphore_signal(
+            barrier, inc=1, device_id={"ep": (me + k) % n}, device_id_type=MESH
+        )
+    pl.semaphore_wait(barrier, n - 1)
 
 
 def forward_kernel(
     tok_ref, cot_ref, routes_ref, rw_ref, wg_hbm, wu_hbm, wd_hbm,
-    gu_ref, hid_ref, x_ref, og_ref, part_ref,
-    w2, wd, blocks, xt, ogt, gut, wsem, send_sem, recv_sem,
+    gu_ref, hid_ref, x_ref, og_ref, grads_ref,
+    w2, wd, blocks, xt, ogt, gut, mine, pair_out, pair_in, out_blocks, in_blocks,
+    wsem, send_sem, recv_sem, pair_send, pair_recv, out_sem, in_sem,
 ):
     me = lax.axis_index("ep")
     expert = me // (lax.axis_size("ep") // EXPERTS)
@@ -174,12 +157,22 @@
     for i in range(parts):
         for one in weight_copies(i):
             one.start()
-    greet()
+    greet(n)
 
     lane = lax.broadcasted_iota(jnp.int32, (rows, LANES), 1)
-    table = jnp.zeros((rows, LANES), F32)
-    for k in range(routes_ref.shape[1]):
-        table += jnp.where(lane == routes_ref[:, k : k + 1], rw_ref[:, k : k + 1].astype(F32), 0.0)
+    number = lax.broadcasted_iota(jnp.int32, (LANES, rows), 0)
+    by_expert = jnp.zeros((LANES, rows), F32)
+    for k in range(routes_ref.shape[0]):
+        by_expert += jnp.where(
+            number == routes_ref[k : k + 1, :], rw_ref[k : k + 1, :].astype(F32), 0.0
+        )
+    same = lax.broadcasted_iota(jnp.int32, (rows, rows), 0) == lax.broadcasted_iota(
+        jnp.int32, (rows, rows), 1
+    )
+    table = lax.dot_general(
+        same.astype(BF16), by_expert.astype(BF16), (((1,), (1,)), ((), ())),
+        preferred_element_type=F32,
+    )
     own = jnp.concatenate([tok_ref[...].astype(F32), cot_ref[...].astype(F32)], axis=0)
     blocks[me, :, :width] = own.astype(BF16)
     blocks[me, :, width:] = jnp.concatenate([table, table], axis=0).astype(BF16)
@@ -223,12 +216,69 @@
 
     lax.fori_loop(0, parts, forward, 0)
 
-    def back(j, carry):
-        cols = pl.ds(pl.multiple_of(j * NCOL, NCOL), NCOL)
-        part_ref[:, cols] = jnp.dot(gut[...], w2[:, cols], preferred_element_type=F32)
+    c = me % 2
+    sibling = me + 1 - 2 * c
+    steps = width // (2 * HALF)
+    fold = HALF // 2
+
+    def pair_copy(s):
+        return pltpu.make_async_remote_copy(
+            src_ref=pair_out.at[s],
+            dst_ref=pair_in.at[s],
+            send_sem=pair_send.at[s],
+            recv_sem=pair_recv.at[s],
+            device_id={"ep": sibling},
+            device_id_type=MESH,
+        )
+
+    def owner_copy(s, owner, source):
+        return pltpu.make_async_remote_copy(
+            src_ref=out_blocks.at[s, owner],
+            dst_ref=in_blocks.at[s, source],
+            send_sem=out_sem.at[s, owner],
+            recv_sem=in_sem.at[s, source],
+            device_id={"ep": owner},
+            device_id_type=MESH,
+        )
+
+    def columns(s, parity):
+        start = pl.multiple_of((2 * s + parity) * HALF, HALF)
+        return jnp.dot(gut[...], w2[:, pl.ds(start, HALF)], preferred_element_type=F32)
+
+    def back(s, carry):
+        pair_out[s] = columns(s, 1 - c)
+        pair_copy(s).start()
+        mine[...] = columns(s, c)
+        pair_copy(s).wait_recv()
+        for b in range(n):
+            at = slice(b * rows, (b + 1) * rows)
+            block = mine[at, :] + pair_in[s, at, :]
+            out_blocks[s, b] = jnp.concatenate([block[:, :fold], block[:, fold:]], axis=0).astype(BF16)
+        for k in range(1, n):
+            owner_copy(s, (me + k) % n, me).start()
+        in_blocks[s, me] = out_blocks[s, me]
         return carry
 
-    lax.fori_loop(0, width // NCOL, back, 0)
+    lax.fori_loop(0, steps, back, 0)
+
+    for s in range(steps):
+        for k in range(1, n):
+            owner_copy(s, me, (me + k) % n).wait_recv()
+        for parity in range(2):
+            total = in_blocks[s, parity].astype(F32)
+            for q in range(1, n // 2):
+                total += in_blocks[s, 2 * q + parity].astype(F32)
+            start = (2 * s + parity) * HALF
+            grads_ref[:, start : start + fold] = total[:rows].astype(BF16)
+            grads_ref[:, start + fold : start + HALF] = total[rows:].astype(BF16)
+
+    def finish(s, carry):
+        pair_copy(s).wait_send()
+        for k in range(1, n):
+            owner_copy(s, (me + k) % n, me).wait_send()
+        return carry
+
+    lax.fori_loop(0, steps, finish, 0)
     drain()
 
 
@@ -246,6 +296,7 @@
     hidden = w_gate.shape[0]
     total = n * rows
     parts = hidden // CHUNK
+    steps = width // (2 * HALF)
     vmem = pl.BlockSpec(memory_space=pltpu.VMEM)
     hbm = pl.BlockSpec(memory_space=pl.ANY)
     return pl.pallas_call(
@@ -255,7 +306,7 @@
             jax.ShapeDtypeStruct((hidden, total), BF16),
             jax.ShapeDtypeStruct((total, width), BF16),
             jax.ShapeDtypeStruct((total, width), BF16),
-            jax.ShapeDtypeStruct((total, width), F32),
+            jax.ShapeDtypeStruct((rows, width), BF16),
         ),
         in_specs=[vmem] * 4 + [hbm] * 3,
         out_specs=(vmem,) * 5,
@@ -266,15 +317,24 @@
             pltpu.VMEM((width, total), BF16),
             pltpu.VMEM((width, total), BF16),
             pltpu.VMEM((total, 2 * hidden), BF16),
+            pltpu.VMEM((total, HALF), F32),
+            pltpu.VMEM((steps, total, HALF), F32),
+            pltpu.VMEM((steps, total, HALF), F32),
+            pltpu.VMEM((steps, n, 2 * rows, HALF // 2), BF16),
+            pltpu.VMEM((steps, n, 2 * rows, HALF // 2), BF16),
             pltpu.SemaphoreType.DMA((3, parts)),
             pltpu.SemaphoreType.DMA((4, n)),
             pltpu.SemaphoreType.DMA((n,)),
+            pltpu.SemaphoreType.DMA((steps,)),
+            pltpu.SemaphoreType.DMA((steps,)),
+            pltpu.SemaphoreType.DMA((steps, n)),
+            pltpu.SemaphoreType.DMA((steps, n)),
         ],
         compiler_params=pltpu.CompilerParams(
             collective_id=0, has_side_effects=True, vmem_limit_bytes=63 * 1024 * 1024
         ),
         name="gather_forward",
-    )(tokens, cotangent, routes, route_weights, w_gate, w_up, w_down)
+    )(tokens, cotangent, routes.T, route_weights.T, w_gate, w_up, w_down)
 
 
 def outer_call(gu, hid, x, og):
@@ -294,7 +354,7 @@
             whole,
         ],
         out_specs=(out,) * 3,
-        compiler_params=pltpu.CompilerParams(vmem_limit_bytes=48 * 1024 * 1024),
+        compiler_params=pltpu.CompilerParams(vmem_limit_bytes=63 * 1024 * 1024),
         cost_estimate=pl.CostEstimate(
             flops=6 * hidden * total * width,
             bytes_accessed=6 * hidden * width + 4 * total * width,
@@ -305,12 +365,11 @@
 
 
 def fused_body(tokens, cotangent, routes, route_weights, w_gate, w_up, w_down):
-    gu, hid, x, og, partial_grads = forward_call(
+    gu, hid, x, og, token_grads = forward_call(
         tokens, cotangent, routes, route_weights, w_gate, w_up, w_down
     )
-    token_grads = lax.psum_scatter(partial_grads, "ep", scatter_dimension=0, tiled=True)
     grad_gate, grad_up, grad_down = outer_call(gu, hid, x, og)
-    return token_grads.astype(BF16), grad_gate, grad_up, grad_down
+    return token_grads, grad_gate, grad_up, grad_down
 
 
 def route_table(routes, route_weights):

time: 123 us -> 73.5 us (0.60)
  waiting for transfers between devices: 35.2 us -> 0 us
  between operations: 14 us -> 0.65 us
  Pallas kernels: 64.1 us -> 72 us
  local copies, waits for them, and re-layouts: 7.39 us -> 0.62 us
  other arithmetic: 1.52 us -> 0 us
    reduce_scatter x1 -> x0, waiting for transfers between devices: 35.2 us -> none  [fused_body(): lax.psum_scatter(partial_grads, 'ep', scatter_dimension=0, tiled=True)]
    pallas_call x1, Pallas kernels: 45.6 us -> 53.3 us  [forward_call(): pl.pallas_call(forward_kernel, out_shape=(jax.ShapeDtypeStruct((2 * hidde...]
    unnamed x10 -> x3, local copies, waits for them, and re-layouts: 7.39 us -> 0.62 us
    convert_element_type x1 -> x0, other arithmetic: 1.52 us -> none  [fused_body(): return (token_grads.astype(BF16), grad_gate, grad_up, grad_down)]
  transfers between devices with their start and end apart: 1 -> 0, of which waited for: 1 -> 0; matrix products, arithmetic and copies ran while one was open for 0% -> 0% of each run, Pallas kernels for 15% -> 0%
where the time goes in v2:
time: 73.5 us; the launch traced here: 73.3 us
  Pallas kernels  72 us (98%)
    pallas_call x1, Pallas kernels, forward_call(): pl.pallas_call(forward_kernel, out_shape=(jax.ShapeDtypeStruct((2 * hidde...  53.3 us
    pallas_call x1, Pallas kernels, outer_call(): pl.pallas_call(outer_kernel, grid=(hidden // OUT_ROWS,), out_shape=(shape...  18.7 us

profile of v2, /device:TPU:0, one launch (start us, length us, event | category | flops | bytes accessed | tf_op | source)
XLA Modules:
  0.0 73.3 jit_solution(11725956317431036624)
XLA Ops:
  0.6 53.3 %gather_forward.1 = (bf16[5376,128]{1,0:T(8,128)(2,1)}, bf16[2688,128]{1,0:T(8,128)(2,1)}, bf16[128,3072]{1,0:T(8,128)(2,1)}, bf16[128,3072]{1,0:T(8,128)(2,1)}, bf16[8,3072]{1,0:T(8,128)(2,1)}) custom-call(bf16[8,3072]{1,0:T(8,128)(2,1)} %tok_ref.1, bf16[8,3072]{1,0:T(8,128)(2,1)} %cot_ref.1, s32[4,8]{1,0:T(4,128)} %bitcast.2, bf16[4,8]{1,0:T(4,128)(2,1)} %bitcast.3, ...), custom_call_target="tpu_custom_call" | custom-call | tf_op jit(solution)/shard_map/gather_forward/pallas_call | solution.py:302
  53.9 0.0 copy-start
  53.9 18.7 %weight_grads.1 = (bf16[2688,3072]{1,0:T(8,128)(2,1)}, bf16[2688,3072]{1,0:T(8,128)(2,1)}, bf16[2688,3072]{1,0:T(8,128)(2,1)}) custom-call(bf16[5376,128]{1,0:T(8,128)(2,1)} %get-tuple-element.13.gu_ref, bf16[2688,128]{1,0:T(8,128)(2,1)} %get-tuple-element.14.hid_ref, bf16[128,3072]{1,0:T(8,128)(2,1)} %get-tuple-element.15.x_ref, ...), custom_call_target="tpu_custom_call" | custom-call | flops 6341787648 | bytes 51118080 | tf_op jit(solution)/shard_map/weight_grads/pallas_call | solution.py:346
  72.7 0.0 copy-done
  72.7 0.6 copy.12
Async XLA Ops:
  53.9 18.8 %copy-start = (bf16[8,3072]{1,0:T(8,128)(2,1)S(1)}, bf16[8,3072]{1,0:T(8,128)(2,1)}, u32[]{:S(2)}) copy-start(bf16[8,3072]{1,0:T(8,128)(2,1)} %get-tuple-element.24) | copy-start | bytes 147460

commit v3 on v2

--- a/solution.py
+++ b/solution.py
@@ -11,7 +11,7 @@
 LANES = 128
 CHUNK = 384
 HALF = 512
-OUT_ROWS = 384
+OUT_COLS = 512
 MESH = pl.DeviceIdType.MESH
 F32 = jnp.float32
 BF16 = jnp.bfloat16
@@ -24,7 +24,6 @@
     def place(zz, yy, cc):
         return (zz * 2 + yy) * 2 + cc
 
-    up, down = place(z + 1, y, c), place(z - 1, y, c)
     across, sibling = place(z, 1 - y, c), place(z, y, 1 - c)
 
     def copy(kind, slot, target):
@@ -38,87 +37,41 @@
         )
 
     def landed(slot):
-        copy(0, slot, sibling).wait_recv()
-
-    def relay_from_below(slot):
-        @pl.when(z < 3)
-        def _():
-            copy(1, slot, up).start()
-
-    def relay_from_above(slot):
-        @pl.when(z > 0)
-        def _():
-            copy(2, slot, down).start()
+        copy(0, slot, across).wait_recv()
 
     def spread(slot):
-        copy(3, slot, across).start()
+        copy(4, slot, across).start()
         copy(0, slot, sibling).start()
 
-    def crossed(zz):
-        slot = place(zz, 1 - y, c)
+    def begin():
+        for d in (1, 2, 3):
+            copy(d, me, place((z + d) % 4, y, c)).start()
+        spread(me)
+
+    def hop(d):
+        slot = place((z + d) % 4, y, c)
+        landed(slot)
+        spread(slot)
+
+    def cross(d):
+        slot = place((z + d) % 4, 1 - y, c)
         landed(slot)
         copy(0, slot, sibling).start()
 
-    relay_from_below(me)
-    relay_from_above(me)
-    spread(me)
-    for d in (1, 2, 3):
-
-        @pl.when(z >= d)
-        def _():
-            slot = place(z - d, y, c)
-            landed(slot)
-            relay_from_below(slot)
-            spread(slot)
-
-        @pl.when(z + d <= 3)
-        def _():
-            slot = place(z + d, y, c)
-            landed(slot)
-            relay_from_above(slot)
-            spread(slot)
-
-        if d == 1:
-            crossed(z)
-        else:
-
-            @pl.when(z >= d - 1)
-            def _():
-                crossed(z - (d - 1))
-
-            @pl.when(z + d - 1 <= 3)
-            def _():
-                crossed(z + d - 1)
-
-    @pl.when(z >= 3)
-    def _():
-        crossed(z - 3)
-
-    @pl.when(z <= 0)
-    def _():
-        crossed(z + 3)
-
-    for zz in range(4):
-        for yy in range(2):
-            landed(place(zz, yy, 1 - c))
+    def finish():
+        for zz in range(4):
+            for yy in range(2):
+                landed(place(zz, yy, 1 - c))
 
     def drain():
+        for d in (1, 2, 3):
+            copy(d, me, place((z + d) % 4, y, c)).wait_send()
         for zz in range(4):
-            slot = place(zz, y, c)
-
-            @pl.when((zz <= z) & (z < 3))
-            def _():
-                copy(1, slot, up).wait_send()
-
-            @pl.when((zz >= z) & (z > 0))
-            def _():
-                copy(2, slot, down).wait_send()
-
-            copy(3, slot, across).wait_send()
-            copy(0, slot, sibling).wait_send()
+            copy(4, place(zz, y, c), across).wait_send()
+            copy(0, place(zz, y, c), sibling).wait_send()
             copy(0, place(zz, 1 - y, c), sibling).wait_send()
 
-    return drain
+    return begin, hop, cross, finish, drain
 
 
 def greet(n):
@@ -133,16 +86,18 @@
 
 def forward_kernel(
     tok_ref, cot_ref, routes_ref, rw_ref, wg_hbm, wu_hbm, wd_hbm,
-    gu_ref, hid_ref, x_ref, og_ref, grads_ref,
-    w2, wd, blocks, xt, ogt, gut, mine, pair_out, pair_in, out_blocks, in_blocks,
-    wsem, send_sem, recv_sem, pair_send, pair_recv, out_sem, in_sem,
+    gg_ref, ug_ref, hid_ref, x_ref, og_ref, grads_ref,
+    w2, wd, tok_blocks, cot_blocks, pre, xt, ogt, gut, mine, pair_out, pair_in, out_blocks, in_blocks,
+    summed, swapped, tab, slot_gut,
+    wsem, tok_send, tok_recv, cot_send, cot_recv, pair_send, pair_recv, out_sem, in_sem, swap_sem,
 ):
     me = lax.axis_index("ep")
     expert = me // (lax.axis_size("ep") // EXPERTS)
     rows, width = tok_ref.shape
     hidden = wd.shape[0]
     parts = hidden // CHUNK
-    n = blocks.shape[0]
+    n = tok_blocks.shape[0]
+    half = width // 2
 
     def weight_copies(i):
         at = pl.multiple_of(i * CHUNK, CHUNK)
@@ -155,8 +110,10 @@
         )
 
     for i in range(parts):
-        for one in weight_copies(i):
+        for one in weight_copies(i)[:2]:
             one.start()
+    for i in range(parts):
+        weight_copies(i)[2].start()
     greet(n)
 
     lane = lax.broadcasted_iota(jnp.int32, (rows, LANES), 1)
@@ -173,45 +130,80 @@
         same.astype(BF16), by_expert.astype(BF16), (((1,), (1,)), ((), ())),
         preferred_element_type=F32,
     )
-    own = jnp.concatenate([tok_ref[...].astype(F32), cot_ref[...].astype(F32)], axis=0)
-    blocks[me, :, :width] = own.astype(BF16)
-    blocks[me, :, width:] = jnp.concatenate([table, table], axis=0).astype(BF16)
-
-    drain = gather_blocks(blocks, send_sem, recv_sem)
+    tok = tok_ref[...].astype(F32)
+    cot = cot_ref[...].astype(F32)
+    tok_blocks[me] = jnp.concatenate([tok[:, :half], tok[:, half:]], axis=0).astype(BF16)
+    cot_blocks[me, :, :half] = jnp.concatenate([cot[:, :half], cot[:, half:]], axis=0).astype(BF16)
+    cot_blocks[me, :, half:] = jnp.concatenate([table, table], axis=0).astype(BF16)
+
+    begin, hop, cross, finish, tok_drain = gather_blocks(tok_blocks, tok_send, tok_recv)
+    cot_begin, cot_hop, cot_cross, cot_finish, cot_drain = gather_blocks(
+        cot_blocks, cot_send, cot_recv
+    )
+    begin()
+    cross(0)
+    for d in (1, 2, 3):
+        hop(d)
+    cot_begin()
+    for d in (1, 2, 3):
+        cross(d)
+    finish()
+
+    def unfold(block):
+        return jnp.concatenate([block[:rows, :half], block[rows:, :half]], axis=1)
 
     for pair in range(n // 2):
-        toks, ogs = [], []
-        for b in (2 * pair, 2 * pair + 1):
-            block = blocks[b].astype(F32)
-            toks.append(block[:rows, :width])
-            coef = jnp.sum(
-                jnp.where(lane == expert, block[rows:, width:], 0.0), axis=1, keepdims=True
-            )
-            ogs.append(coef * block[rows:, :width])
         at = slice(2 * rows * pair, 2 * rows * (pair + 1))
+        toks = [unfold(tok_blocks[b].astype(F32)) for b in (2 * pair, 2 * pair + 1)]
         x_ref[at, :] = jnp.concatenate(toks, axis=0).astype(BF16)
-        og_ref[at, :] = jnp.concatenate(ogs, axis=0).astype(BF16)
     for j in range(0, width, 512):
         xt[j : j + 512, :] = x_ref[:, j : j + 512].T
+
+    def pre_activations(i, carry):
+        for one in weight_copies(i)[:2]:
+            one.wait()
+        both = pl.ds(pl.multiple_of(i * 2 * CHUNK, CHUNK), 2 * CHUNK)
+        pre[both, :] = jnp.dot(w2[both, :], xt[...], preferred_element_type=F32)
+        for d in (1, 2, 3):
+            pl.when(i == 1)(functools.partial(cot_hop, d))
+        for d in range(4):
+            pl.when(i == 3)(functools.partial(cot_cross, d))
+        return carry
+
+    lax.fori_loop(0, parts, pre_activations, 0)
+    cot_finish()
+
+    for pair in range(n // 2):
+        ogs, tables = [], []
+        for b in (2 * pair, 2 * pair + 1):
+            block = cot_blocks[b].astype(F32)
+            coef = jnp.sum(
+                jnp.where(lane == expert, block[:rows, half:], 0.0), axis=1, keepdims=True
+            )
+            ogs.append(coef * unfold(block))
+            tables.append(block[:rows, half:])
+        at = slice(2 * rows * pair, 2 * rows * (pair + 1))
+        og_ref[at, :] = jnp.concatenate(ogs, axis=0).astype(BF16)
+        tab[at, :] = jnp.concatenate(tables, axis=0).astype(BF16)
+    for j in range(0, width, 512):
         ogt[j : j + 512, :] = og_ref[:, j : j + 512].T
 
     def forward(i, carry):
-        for one in weight_copies(i):
-            one.wait()
+        weight_copies(i)[2].wait()
         at = pl.ds(pl.multiple_of(i * CHUNK, CHUNK), CHUNK)
         low = pl.multiple_of(i * 2 * CHUNK, CHUNK)
-        both = jnp.dot(w2[pl.ds(low, 2 * CHUNK), :], xt[...], preferred_element_type=F32)
-        gate, up = both[:CHUNK], both[CHUNK:]
+        high = pl.multiple_of(low + CHUNK, CHUNK)
+        gate, up = pre[pl.ds(low, CHUNK), :], pre[pl.ds(high, CHUNK), :]
         hgrad = jnp.dot(wd[at, :], ogt[...], preferred_element_type=F32)
         sig = 1.0 / (1.0 + jnp.exp(-gate))
         act = gate * sig
         hid_ref[at, :] = (act * up).astype(BF16)
         up_grad = (hgrad * act).astype(BF16)
         gate_grad = (hgrad * up * sig * (1.0 + gate * (1.0 - sig))).astype(BF16)
-        gu_ref[pl.ds(low, CHUNK), :] = gate_grad
-        gu_ref[pl.ds(low + CHUNK, CHUNK), :] = up_grad
+        gg_ref[at, :] = gate_grad
+        ug_ref[at, :] = up_grad
         gut[:, pl.ds(low, CHUNK)] = gate_grad.T
-        gut[:, pl.ds(low + CHUNK, CHUNK)] = up_grad.T
+        gut[:, pl.ds(high, CHUNK)] = up_grad.T
         return carry
 
     lax.fori_loop(0, parts, forward, 0)
@@ -220,6 +212,29 @@
     sibling = me + 1 - 2 * c
     steps = width // (2 * HALF)
     fold = HALF // 2
+    total_rows = n * rows
+
+    def iota(shape, dim):
+        return lax.broadcasted_iota(jnp.int32, shape, dim)
+
+    pick = (iota((8, LANES), 1) == expert).astype(BF16)
+    weight = lax.dot_general(
+        pick, tab[...], (((1,), (1,)), ((), ())), preferred_element_type=F32
+    )
+    named = jnp.where(weight > 0.0, 1.0, 0.0)
+    square = (total_rows, total_rows)
+    before = (iota(square, 0) < iota(square, 1)) & (
+        lax.div(iota(square, 0), rows) == lax.div(iota(square, 1), rows)
+    )
+    rank = jnp.dot(named.astype(BF16), before.astype(BF16), preferred_element_type=F32)
+    wide = (n * CAP, total_rows)
+    fits = (lax.div(iota(wide, 0), CAP) == lax.div(iota(wide, 1), rows)) & (
+        rank[:1] == lax.rem(iota(wide, 0), CAP).astype(F32)
+    )
+    select = jnp.where(fits, named[:1], 0.0).astype(BF16)
+    for j in range(0, 2 * hidden, 2 * CHUNK):
+        cut = slice(j, j + 2 * CHUNK)
+        slot_gut[:, cut] = jnp.dot(select, gut[:, cut], preferred_element_type=F32).astype(BF16)
 
     def pair_copy(s):
         return pltpu.make_async_remote_copy(
@@ -231,63 +246,100 @@
             device_id_type=MESH,
         )
 
-    def owner_copy(s, owner, source):
+    chips = n // 2
+    chip = me // 2
+
+    def chip_copy(s, to, source):
         return pltpu.make_async_remote_copy(
-            src_ref=out_blocks.at[s, owner],
+            src_ref=out_blocks.at[s, to],
             dst_ref=in_blocks.at[s, source],
-            send_sem=out_sem.at[s, owner],
+            send_sem=out_sem.at[s, to],
             recv_sem=in_sem.at[s, source],
-            device_id={"ep": owner},
+            device_id={"ep": 2 * to + c},
             device_id_type=MESH,
         )
 
     def columns(s, parity):
         start = pl.multiple_of((2 * s + parity) * HALF, HALF)
-        return jnp.dot(gut[...], w2[:, pl.ds(start, HALF)], preferred_element_type=F32)
+        return jnp.dot(slot_gut[...], w2[:, pl.ds(start, HALF)], preferred_element_type=F32)
 
     def back(s, carry):
         pair_out[s] = columns(s, 1 - c)
         pair_copy(s).start()
         mine[...] = columns(s, c)
         pair_copy(s).wait_recv()
-        for b in range(n):
-            at = slice(b * rows, (b + 1) * rows)
+        for q in range(chips):
+            at = slice(2 * q * CAP, 2 * (q + 1) * CAP)
             block = mine[at, :] + pair_in[s, at, :]
-            out_blocks[s, b] = jnp.concatenate([block[:, :fold], block[:, fold:]], axis=0).astype(BF16)
-        for k in range(1, n):
-            owner_copy(s, (me + k) % n, me).start()
-        in_blocks[s, me] = out_blocks[s, me]
+            out_blocks[s, q] = jnp.concatenate([block[:, :fold], block[:, fold:]], axis=0).astype(BF16)
+        for k in range(1, chips):
+            chip_copy(s, (chip + k) % chips, chip).start()
+        in_blocks[s, chip] = out_blocks[s, chip]
         return carry
 
     lax.fori_loop(0, steps, back, 0)
 
+    source = chips * 4 * CAP
+    spot = iota((rows, source), 1)
+    slot_of = lax.rem(spot, CAP).astype(F32)
+    earlier = (iota((rows, rows), 0) > iota((rows, rows), 1)).astype(BF16)
+    spread_out = (iota((LANES, source), 0) == lax.div(iota((LANES, source), 1), 4 * CAP)).astype(BF16)
+    expand = []
+    for owner in range(2):
+        held = cot_blocks[2 * chip + owner].astype(F32)[:rows, half:]
+        names = jnp.where(held > 0.0, 1.0, 0.0).astype(BF16)
+        ranks = jnp.dot(earlier, names, preferred_element_type=F32).astype(BF16)
+        names = jnp.dot(names, spread_out, preferred_element_type=F32)
+        ranks = jnp.dot(ranks, spread_out, preferred_element_type=F32)
+        for part in range(2):
+            ours = lax.rem(lax.div(spot, CAP), 4) == 2 * part + owner
+            expand.append(jnp.where(ours & (ranks == slot_of), names, 0.0))
+    expand = jnp.concatenate(expand, axis=0).astype(BF16)
+
     for s in range(steps):
-        for k in range(1, n):
-            owner_copy(s, me, (me + k) % n).wait_recv()
-        for parity in range(2):
-            total = in_blocks[s, parity].astype(F32)
-            for q in range(1, n // 2):
-                total += in_blocks[s, 2 * q + parity].astype(F32)
-            start = (2 * s + parity) * HALF
-            grads_ref[:, start : start + fold] = total[:rows].astype(BF16)
-            grads_ref[:, start + fold : start + HALF] = total[rows:].astype(BF16)
-
-    def finish(s, carry):
+        for k in range(1, chips):
+            chip_copy(s, chip, (chip + k) % chips).wait_recv()
+        arrived = in_blocks[s].reshape(source, fold)
+        total = jnp.dot(expand, arrived, preferred_element_type=F32)
+        summed[0, s] = total[: 2 * rows].astype(BF16)
+        summed[1, s] = total[2 * rows :].astype(BF16)
+
+    swap = pltpu.make_async_remote_copy(
+        src_ref=summed.at[1 - c],
+        dst_ref=swapped,
+        send_sem=swap_sem.at[0],
+        recv_sem=swap_sem.at[1],
+        device_id={"ep": sibling},
+        device_id_type=MESH,
+    )
+    swap.start()
+
+    def place_columns(s, parity, block):
+        block = block.astype(F32)
+        flat = jnp.concatenate([block[:rows], block[rows:]], axis=1)
+        start = pl.multiple_of((2 * s + parity) * HALF, HALF)
+        grads_ref[:, pl.ds(start, HALF)] = flat.astype(BF16)
+
+    for s in range(steps):
+        place_columns(s, c, summed[c, s])
+    for s in range(steps):
         pair_copy(s).wait_send()
-        for k in range(1, n):
-            owner_copy(s, (me + k) % n, me).wait_send()
-        return carry
-
-    lax.fori_loop(0, steps, finish, 0)
-    drain()
-
-
-def outer_kernel(gu_ref, hid_ref, x_ref, og_ref, gate_out, up_out, down_out):
-    half = gate_out.shape[0]
-    both = jnp.dot(gu_ref[...], x_ref[...], preferred_element_type=F32).astype(BF16)
-    gate_out[...] = both[:half]
-    up_out[...] = both[half:]
-    down_out[...] = jnp.dot(hid_ref[...], og_ref[...], preferred_element_type=F32).astype(BF16)
+        for k in range(1, chips):
+            chip_copy(s, (chip + k) % chips, chip).wait_send()
+    swap.wait()
+    for s in range(steps):
+        place_columns(s, 1 - c, swapped[s])
+    tok_drain()
+    cot_drain()
+
+
+def outer_kernel(gg_ref, ug_ref, hid_ref, x_ref, og_ref, gate_out, up_out, down_out):
+    for left, right, out in (
+        (gg_ref, x_ref, gate_out),
+        (ug_ref, x_ref, up_out),
+        (hid_ref, og_ref, down_out),
+    ):
+        out[...] = jnp.dot(left[...], right[...], preferred_element_type=F32).astype(BF16)
 
 
 def forward_call(tokens, cotangent, routes, route_weights, w_gate, w_up, w_down):
@@ -302,33 +354,43 @@
     return pl.pallas_call(
         forward_kernel,
         out_shape=(
-            jax.ShapeDtypeStruct((2 * hidden, total), BF16),
+            jax.ShapeDtypeStruct((hidden, total), BF16),
+            jax.ShapeDtypeStruct((hidden, total), BF16),
             jax.ShapeDtypeStruct((hidden, total), BF16),
             jax.ShapeDtypeStruct((total, width), BF16),
             jax.ShapeDtypeStruct((total, width), BF16),
             jax.ShapeDtypeStruct((rows, width), BF16),
         ),
         in_specs=[vmem] * 4 + [hbm] * 3,
-        out_specs=(vmem,) * 5,
+        out_specs=(vmem,) * 6,
         scratch_shapes=[
             pltpu.VMEM((2 * hidden, width), BF16),
             pltpu.VMEM((hidden, width), BF16),
-            pltpu.VMEM((n, 2 * rows, width + LANES), BF16),
+            pltpu.VMEM((n, 2 * rows, width // 2), BF16),
+            pltpu.VMEM((n, 2 * rows, width // 2 + LANES), BF16),
+            pltpu.VMEM((2 * hidden, total), F32),
             pltpu.VMEM((width, total), BF16),
             pltpu.VMEM((width, total), BF16),
             pltpu.VMEM((total, 2 * hidden), BF16),
-            pltpu.VMEM((total, HALF), F32),
-            pltpu.VMEM((steps, total, HALF), F32),
-            pltpu.VMEM((steps, total, HALF), F32),
-            pltpu.VMEM((steps, n, 2 * rows, HALF // 2), BF16),
-            pltpu.VMEM((steps, n, 2 * rows, HALF // 2), BF16),
+            pltpu.VMEM((n * CAP, HALF), F32),
+            pltpu.VMEM((steps, n * CAP, HALF), F32),
+            pltpu.VMEM((steps, n * CAP, HALF), F32),
+            pltpu.VMEM((steps, n // 2, 4 * CAP, HALF // 2), BF16),
+            pltpu.VMEM((steps, n // 2, 4 * CAP, HALF // 2), BF16),
+            pltpu.VMEM((2, steps, 2 * rows, HALF // 2), BF16),
+            pltpu.VMEM((steps, 2 * rows, HALF // 2), BF16),
+            pltpu.VMEM((total, LANES), BF16),
+            pltpu.VMEM((n * CAP, 2 * hidden), BF16),
             pltpu.SemaphoreType.DMA((3, parts)),
-            pltpu.SemaphoreType.DMA((4, n)),
+            pltpu.SemaphoreType.DMA((5, n)),
+            pltpu.SemaphoreType.DMA((n,)),
+            pltpu.SemaphoreType.DMA((5, n)),
             pltpu.SemaphoreType.DMA((n,)),
             pltpu.SemaphoreType.DMA((steps,)),
             pltpu.SemaphoreType.DMA((steps,)),
-            pltpu.SemaphoreType.DMA((steps, n)),
-            pltpu.SemaphoreType.DMA((steps, n)),
+            pltpu.SemaphoreType.DMA((steps, n // 2)),
+            pltpu.SemaphoreType.DMA((steps, n // 2)),
+            pltpu.SemaphoreType.DMA((2,)),
         ],
         compiler_params=pltpu.CompilerParams(
             collective_id=0, has_side_effects=True, vmem_limit_bytes=63 * 1024 * 1024
@@ -337,22 +399,18 @@
     )(tokens, cotangent, routes.T, route_weights.T, w_gate, w_up, w_down)
 
 
-def outer_call(gu, hid, x, og):
+def outer_call(gg, ug, hid, x, og):
     hidden, total = hid.shape
     width = x.shape[1]
-    whole = pl.BlockSpec((total, width), lambda i: (0, 0))
-    out = pl.BlockSpec((OUT_ROWS, width), lambda i: (i, 0))
+    rows = pl.BlockSpec((hidden, total), lambda i: (0, 0))
+    narrow = pl.BlockSpec((total, OUT_COLS), lambda i: (0, i))
+    out = pl.BlockSpec((hidden, OUT_COLS), lambda i: (0, i))
     shape = jax.ShapeDtypeStruct((hidden, width), BF16)
     return pl.pallas_call(
         outer_kernel,
-        grid=(hidden // OUT_ROWS,),
+        grid=(width // OUT_COLS,),
         out_shape=(shape,) * 3,
-        in_specs=[
-            pl.BlockSpec((2 * OUT_ROWS, total), lambda i: (i, 0)),
-            pl.BlockSpec((OUT_ROWS, total), lambda i: (i, 0)),
-            whole,
-            whole,
-        ],
+        in_specs=[rows, rows, rows, narrow, narrow],
         out_specs=(out,) * 3,
         compiler_params=pltpu.CompilerParams(vmem_limit_bytes=63 * 1024 * 1024),
         cost_estimate=pl.CostEstimate(
@@ -361,14 +419,14 @@
             transcendentals=0,
         ),
         name="weight_grads",
-    )(gu, hid, x, og)
+    )(gg, ug, hid, x, og)
 
 
 def fused_body(tokens, cotangent, routes, route_weights, w_gate, w_up, w_down):
-    gu, hid, x, og, token_grads = forward_call(
+    gg, ug, hid, x, og, token_grads = forward_call(
         tokens, cotangent, routes, route_weights, w_gate, w_up, w_down
     )
-    grad_gate, grad_up, grad_down = outer_call(gu, hid, x, og)
+    grad_gate, grad_up, grad_down = outer_call(gg, ug, hid, x, og)
     return token_grads, grad_gate, grad_up, grad_down
 
 

time: 73.5 us -> 73.6 us (level)
  no operation moved by 1% of the time
where the time goes in v3:
time: 73.6 us; the launch traced here: 73.4 us
  Pallas kernels  72.1 us (98%)
    pallas_call x1, Pallas kernels, forward_call(): pl.pallas_call(forward_kernel, out_shape=(jax.ShapeDtypeStruct((hidden, t...  53.8 us
    pallas_call x1, Pallas kernels, outer_call(): pl.pallas_call(outer_kernel, grid=(width // OUT_COLS,), out_shape=(shape,...  18.3 us

profile of v3, /device:TPU:0, one launch (start us, length us, event | category | flops | bytes accessed | tf_op | source)
XLA Modules:
  0.0 73.4 jit_solution(16379607373054653637)
XLA Ops:
  0.6 53.8 %gather_forward.1 = (bf16[2688,128]{1,0:T(8,128)(2,1)}, bf16[2688,128]{1,0:T(8,128)(2,1)}, bf16[2688,128]{1,0:T(8,128)(2,1)}, bf16[128,3072]{1,0:T(8,128)(2,1)},...) custom-call(bf16[8,3072]{1,0:T(8,128)(2,1)} %tok_ref.1, bf16[8,3072]{1,0:T(8,128)(2,1)} %cot_ref.1, s32[4,8]{1,0:T(4,128)} %bitcast.2, ...), custom_call_target="tpu_custom_call" | custom-call | tf_op jit(solution)/shard_map/gather_forward/pallas_call | solution.py:354
  54.5 0.0 copy-start
  54.5 18.3 %weight_grads.1 = (bf16[2688,3072]{1,0:T(8,128)(2,1)}, bf16[2688,3072]{1,0:T(8,128)(2,1)}, bf16[2688,3072]{1,0:T(8,128)(2,1)}) custom-call(bf16[2688,128]{1,0:T(8,128)(2,1)} %get-tuple-element.14.gg_ref, bf16[2688,128]{1,0:T(8,128)(2,1)} %get-tuple-element.15.ug_ref, bf16[2688,128]{1,0:T(8,128)(2,1)} %get-tuple-element.16.hid_ref, ...), custom_call_target="tpu_custom_call" | custom-call | flops 6341787648 | bytes 51118080 | tf_op jit(solution)/shard_map/weight_grads/pallas_call | solution.py:409
  72.8 0.0 copy-done
  72.8 0.6 copy.12
Async XLA Ops:
  54.5 18.3 %copy-start = (bf16[8,3072]{1,0:T(8,128)(2,1)S(1)}, bf16[8,3072]{1,0:T(8,128)(2,1)}, u32[]{:S(2)}) copy-start(bf16[8,3072]{1,0:T(8,128)(2,1)} %get-tuple-element.26) | copy-start | bytes 147460
